TPU v7x, 32 devices: a whole 2x2x4 slice. The times are simulated.
32 devices in a mesh: img: 4 (over z), gx: 2 (over x), gz: 4 (over y, core).
Axes of the slice: x: 2, y: 2, z: 4, core: 2. Of those that a mesh axis runs over, the one named last changes fastest.
Arguments:
- species: float32 [4, 2, 32, 16, 512], P('img', None, 'gx', None, 'gz'), may hold values from -2.5 to 2.5
- diffusion: float32 [2, 32, 16, 512], P(None, 'gx', None, 'gz'), may hold values from 0.1 to 2
- z_inverse: float32 [2, 512, 512], replicated, may hold values from -1 to 1.5
- starts: int32 [4], replicated, may hold values from -1 to 1, as said below
- weights: float32 [4, 4], replicated, may hold values from -0.1 to 1, as said below
Outputs:
- new_string: float32 [4, 2, 32, 16, 512], P('img', None, 'gx', None, 'gz')
Inputs may be any that keep to these rules, and one draw needn't show every extreme that they name: starts[t] is t - 2 or t - 1. Each row holds the cubic Lagrange weights at a point between the second and third of four equally spaced images.
All inputs are finite; a program needn't handle non-finite values.
Results may differ from a plain program's by a relative error of at most 0.00012.
Values sent between devices are 32-bit elements; how exact they have to be, the bound alone decides.
A program may use at most 64 MiB of HBM per device.

v0:
```python
import jax
import jax.numpy as jnp
from jax import lax
from jax.sharding import PartitionSpec as P

STEPS = 4
step_size = 0.05


def with_halo(cells, sides, width):
    for axis, dim in sides:
        count = lax.axis_size(axis)
        ends = count - 1
        head = lax.slice_in_dim(cells, 0, width, axis=dim)
        tail = lax.slice_in_dim(cells, cells.shape[dim] - width, cells.shape[dim], axis=dim)
        cells = jnp.concatenate(
            [
                lax.ppermute(tail, axis, [(i, (i + 1) % count) for i in range(ends)]),
                cells,
                lax.ppermute(head, axis, [((i + 1) % count, i) for i in range(ends)]),
            ],
            axis=dim,
        )
    return cells


def passed_along(value, axis, steps):
    count = lax.axis_size(axis)
    first, last = (max(0, -steps), min(count, count - steps))
    return lax.ppermute(value, axis, [(source, source + steps) for source in range(first, last)])


def reaction(state):
    first = state[0]
    second = state[1]
    return jnp.stack([first - first * first * first - second + 0.2, 0.5 * (first - second)])


def spread_flux(state, padded, coeffs):
    centre = coeffs[:, 1:-1, 1:-1]
    total = (centre + coeffs[:, :-2, 1:-1]) * (padded[:, :-2, 1:-1] - state)
    total = total + (centre + coeffs[:, 2:, 1:-1]) * (padded[:, 2:, 1:-1] - state)
    total = total + (centre + coeffs[:, 1:-1, :-2]) * (padded[:, 1:-1, :-2] - state)
    total = total + (centre + coeffs[:, 1:-1, 2:]) * (padded[:, 1:-1, 2:] - state)
    return 0.5 * total


def local(species, diffusion, z_inverse, starts, weights):
    state = species[0]
    y_widths = ((0, 0), (0, 0), (1, 1), (0, 0))
    coeffs = with_halo(diffusion, (("gx", 1),), 1)
    coeffs = jnp.pad(coeffs, y_widths)
    for repeat in range(STEPS):
        padded = with_halo(state, (("gx", 1),), 1)
        padded = jnp.pad(padded, y_widths)
        source = state + step_size * (reaction(state) + spread_flux(state, padded, coeffs))
        solved = jnp.einsum(
            "sij,sabj->sabi",
            z_inverse,
            lax.all_to_all(source, "gz", split_axis=2, concat_axis=3, tiled=True),
            precision=lax.Precision.HIGHEST,
        )
        state = lax.all_to_all(solved, "gz", split_axis=3, concat_axis=2, tiled=True)
    before_one = passed_along(state, "img", 1)
    before_two = passed_along(state, "img", 2)
    after_one = passed_along(state, "img", -1)
    after_two = passed_along(state, "img", -2)
    images = lax.axis_size("img")
    target = lax.axis_index("img")
    listed = jnp.arange(images, dtype=jnp.int32)
    picked = listed == target
    first_image = jnp.sum(jnp.where(picked, starts, 0))
    my_weights = jnp.sum(jnp.where(picked[:, None], weights, 0.0), axis=0)
    sources = {-2: before_two, -1: before_one, 0: state, 1: after_one, 2: after_two}
    result = None
    for offset in range(-2, 3):
        coef = jnp.zeros((), jnp.float32)
        for place in range(4):
            coef = coef + jnp.where(first_image + place == target + offset, my_weights[place], 0.0)
        term = coef * sources[offset]
        result = term if result is None else result + term
    return result[None]


def solution(mesh):
    return jax.shard_map(
        local,
        mesh=mesh,
        in_specs=(P("img", None, "gx", None, "gz"), P(None, "gx", None, "gz"), P(), P(), P()),
        out_specs=P("img", None, "gx", None, "gz"),
        check_vma=False,
    )
```

profile of v0, /device:TPU:24, one launch (start us, length us, event | category | flops | bytes accessed | tf_op | source)
XLA Modules:
  0.0 201.2 jit_solution(16023715058296012637)
XLA Ops:
  0.9 3.4 %collective-permute-start = (f32[2,1,16,128]{3,1,0,2:T(1,128)S(1)}, f32[2,1,16,128]{3,1,0,2:T(1,128)S(1)}, u32[]{:S(2)}, u32[]{:S(2)}) collective-permute-start(f32[2,1,16,128]{3,1,0,2:T(1,128)S(1)} %copy.23), channel_id=1, source_target_pairs={{0,4},{1,5},{2,6},{3,7},{8,12},{9,13},{10,14},{11,15},{16,20},{17,... | collective-permute-start | bytes 49160 | tf_op jit(solution)/shard_map/ppermute | solution.py:18
  4.4 1.3 collective-permute-start.2
  6.7 4.5 %collective-permute-start.1 = (f32[2,1,16,128]{3,1,0,2:T(1,128)S(1)}, f32[2,1,16,128]{3,1,0,2:T(1,128)S(1)}, u32[]{:S(2)}, u32[]{:S(2)}) collective-permute-start(f32[2,1,16,128]{3,1,0,2:T(1,128)S(1)} %get-tuple-element.32), channel_id=1, source_target_pairs={{0,4},{1,5},{2,6},{3,7},{8,12},{9,13},{10,14},{11,15},{16,20},{17,... | collective-permute-start | bytes 49160 | tf_op jit(solution)/shard_map/ppermute | solution.py:18
  11.3 1.3 collective-permute-start.3
  14.7 2.2 %collective-permute-done.3 = f32[2,1,16,128]{3,1,0,2:T(1,128)S(1)} collective-permute-done((f32[2,1,16,128]{3,1,0,2:T(1,128)S(1)}, f32[2,1,16,128]{3,1,0,2:T(1,128)S(1)}, u32[]{:S(2)}, u32[]{:S(2)}) %collective-permute-start.3) | collective-permute-done | bytes 16416 | tf_op jit(solution)/shard_map/ppermute | solution.py:20
  17.5 8.6 %all_to_all.144 = f32[2,16,16,128]{3,1,0,2:T(8,128)S(1)} all-to-all(f32[2,16,16,128]{3,1,0,2:T(8,128)S(1)} %get-tuple-element.5), channel_id=1, replica_groups=mesh['img'=4,'gx'=2,'gz'=4] {'gz'}, dimensions={2} | all-to-all | bytes 524288 | tf_op jit(solution)/shard_map/all_to_all | solution.py:60
  28.0 2.1 %fusion.6 = f32[2,16,4,512]{3,1,2,0:T(8,128)S(1)} fusion(f32[2,16,4,512]{3,1,2,0:T(8,128)S(1)} %all_to_all.107, f32[2,512,512]{2,1,0:T(8,128)S(1)} %copy-done), kind=kOutput, calls=%fused_computation.6 | convolution fusion | flops 402653184 | bytes 2621440 | tf_op jit(solution)/shard_map/sij,sabj->sabi/dot_general | solution.py:57
  30.2 1.7 copy.33
  31.9 3.1 %reshape.265 = f32[4,1,16384]{2,1,0:T(1,128)S(1)} reshape(f32[512,2,4,16]{3,2,1,0:T(4,128)} %bitcast.108) | data formatting | bytes 524288
  35.0 8.4 %all_to_all.145 = f32[4,1,16384]{2,1,0:T(1,128)S(1)} all-to-all(f32[4,1,16384]{2,1,0:T(1,128)S(1)} %reshape.265), channel_id=1, replica_groups=mesh['img'=4,'gx'=2,'gz'=4] {'gz'}, dimensions={0} | all-to-all | bytes 524288 | tf_op jit(solution)/shard_map/all_to_all | solution.py:63
  44.0 1.4 reduce
  45.4 2.9 %reshape.266 = f32[512,2,4,16]{3,2,1,0:T(4,128)} reshape(f32[4,16384]{1,0:T(4,128)S(1)} %reduce) | data formatting | bytes 524288
  48.3 1.8 copy.34
  50.1 2.4 %collective-permute-start.4 = (f32[2,1,16,128]{3,1,0,2:T(1,128)S(1)}, f32[2,1,16,128]{3,1,0,2:T(1,128)S(1)}, u32[]{:S(2)}, u32[]{:S(2)}) collective-permute-start(f32[2,1,16,128]{3,1,0,2:T(1,128)S(1)} %get-tuple-element.24), channel_id=1, source_target_pairs={{0,4},{1,5},{2,6},{3,7},{8,12},{9,13},{10,14},{11,15},{16,20},{17,... | collective-permute-start | bytes 49160 | tf_op jit(solution)/shard_map/ppermute | solution.py:18
  52.5 1.3 collective-permute-start.5
  53.9 4.2 %collective-permute-done.5 = f32[2,1,16,128]{3,1,0,2:T(1,128)S(1)} collective-permute-done((f32[2,1,16,128]{3,1,0,2:T(1,128)S(1)}, f32[2,1,16,128]{3,1,0,2:T(1,128)S(1)}, u32[]{:S(2)}, u32[]{:S(2)}) %collective-permute-start.5) | collective-permute-done | bytes 16416 | tf_op jit(solution)/shard_map/ppermute | solution.py:20
  58.5 8.4 %all_to_all.146 = f32[2,16,16,128]{3,1,0,2:T(8,128)S(1)} all-to-all(f32[2,16,16,128]{3,1,0,2:T(8,128)S(1)} %fusion.40), channel_id=1, replica_groups=mesh['img'=4,'gx'=2,'gz'=4] {'gz'}, dimensions={2} | all-to-all | bytes 524288 | tf_op jit(solution)/shard_map/all_to_all | solution.py:60
  68.9 2.1 %fusion.4 = f32[2,16,4,512]{3,1,2,0:T(8,128)S(1)} fusion(f32[2,16,4,512]{3,1,2,0:T(8,128)S(1)} %all_to_all.115, f32[2,512,512]{2,1,0:T(8,128)S(1)} %copy-done), kind=kOutput, calls=%fused_computation.4 | convolution fusion | flops 402653184 | bytes 2621440 | tf_op jit(solution)/shard_map/sij,sabj->sabi/dot_general | solution.py:57
  71.0 1.7 copy.36
  72.8 3.1 %reshape.267 = f32[4,1,16384]{2,1,0:T(1,128)S(1)} reshape(f32[512,2,4,16]{3,2,1,0:T(4,128)} %bitcast.110) | data formatting | bytes 524288
  75.8 8.4 %all_to_all.147 = f32[4,1,16384]{2,1,0:T(1,128)S(1)} all-to-all(f32[4,1,16384]{2,1,0:T(1,128)S(1)} %reshape.267), channel_id=1, replica_groups=mesh['img'=4,'gx'=2,'gz'=4] {'gz'}, dimensions={0} | all-to-all | bytes 524288 | tf_op jit(solution)/shard_map/all_to_all | solution.py:63
  84.3 1.4 reduce.1
  85.7 2.9 %reshape.268 = f32[512,2,4,16]{3,2,1,0:T(4,128)} reshape(f32[4,16384]{1,0:T(4,128)S(1)} %reduce.1) | data formatting | bytes 524288
  88.5 1.8 copy.37
  90.4 1.6 collective-permute-start.6
  92.1 1.3 collective-permute-start.7
  93.5 4.2 %collective-permute-done.7 = f32[2,1,16,128]{3,1,0,2:T(1,128)S(1)} collective-permute-done((f32[2,1,16,128]{3,1,0,2:T(1,128)S(1)}, f32[2,1,16,128]{3,1,0,2:T(1,128)S(1)}, u32[]{:S(2)}, u32[]{:S(2)}) %collective-permute-start.7) | collective-permute-done | bytes 16416 | tf_op jit(solution)/shard_map/ppermute | solution.py:20
  98.1 8.4 %all_to_all.148 = f32[2,16,16,128]{3,1,0,2:T(8,128)S(1)} all-to-all(f32[2,16,16,128]{3,1,0,2:T(8,128)S(1)} %fusion.27), channel_id=1, replica_groups=mesh['img'=4,'gx'=2,'gz'=4] {'gz'}, dimensions={2} | all-to-all | bytes 524288 | tf_op jit(solution)/shard_map/all_to_all | solution.py:60
  108.4 2.1 %fusion.2 = f32[2,16,4,512]{3,1,2,0:T(8,128)S(1)} fusion(f32[2,16,4,512]{3,1,2,0:T(8,128)S(1)} %all_to_all.123, f32[2,512,512]{2,1,0:T(8,128)S(1)} %copy-done), kind=kOutput, calls=%fused_computation.2 | convolution fusion | flops 402653184 | bytes 2621440 | tf_op jit(solution)/shard_map/sij,sabj->sabi/dot_general | solution.py:57
  110.6 1.7 copy.39
  112.3 3.1 %reshape.269 = f32[4,1,16384]{2,1,0:T(1,128)S(1)} reshape(f32[512,2,4,16]{3,2,1,0:T(4,128)} %bitcast.112) | data formatting | bytes 524288
  115.4 8.4 %all_to_all.149 = f32[4,1,16384]{2,1,0:T(1,128)S(1)} all-to-all(f32[4,1,16384]{2,1,0:T(1,128)S(1)} %reshape.269), channel_id=1, replica_groups=mesh['img'=4,'gx'=2,'gz'=4] {'gz'}, dimensions={0} | all-to-all | bytes 524288 | tf_op jit(solution)/shard_map/all_to_all | solution.py:63
  123.8 1.4 reduce.2
  125.2 2.9 %reshape.270 = f32[512,2,4,16]{3,2,1,0:T(4,128)} reshape(f32[4,16384]{1,0:T(4,128)S(1)} %reduce.2) | data formatting | bytes 524288
  128.1 1.8 copy.40
  130.0 1.6 collective-permute-start.8
  133.1 4.2 %collective-permute-done.9 = f32[2,1,16,128]{3,1,0,2:T(1,128)S(1)} collective-permute-done((f32[2,1,16,128]{3,1,0,2:T(1,128)S(1)}, f32[2,1,16,128]{3,1,0,2:T(1,128)S(1)}, u32[]{:S(2)}, u32[]{:S(2)}) %collective-permute-start.9) | collective-permute-done | bytes 16416 | tf_op jit(solution)/shard_map/ppermute | solution.py:20
  137.6 8.4 %all_to_all.150 = f32[2,16,16,128]{3,1,0,2:T(8,128)S(1)} all-to-all(f32[2,16,16,128]{3,1,0,2:T(8,128)S(1)} %fusion.14), channel_id=1, replica_groups=mesh['img'=4,'gx'=2,'gz'=4] {'gz'}, dimensions={2} | all-to-all | bytes 524288 | tf_op jit(solution)/shard_map/all_to_all | solution.py:60
  146.3 2.1 %fusion = f32[2,16,4,512]{3,1,2,0:T(8,128)S(1)} fusion(f32[2,16,4,512]{3,1,2,0:T(8,128)S(1)} %all_to_all.131, f32[2,512,512]{2,1,0:T(8,128)S(1)} %copy-done), kind=kOutput, calls=%fused_computation | convolution fusion | flops 402653184 | bytes 2621440 | tf_op jit(solution)/shard_map/sij,sabj->sabi/dot_general | solution.py:57
  148.5 1.7 copy.42
  150.2 3.7 %reshape.271 = f32[4,1,16384]{2,1,0:T(1,128)} reshape(f32[512,2,4,16]{3,2,1,0:T(4,128)} %bitcast.114) | data formatting | bytes 524288
  153.9 3.4 %all-to-all-start.7 = ((f32[4,1,16384]{2,1,0:T(1,128)}), f32[4,1,16384]{2,1,0:T(1,128)S(1)}, u32[]{:S(2)}, u32[]{:S(2)}) async-start(f32[4,1,16384]{2,1,0:T(1,128)} %reshape.271), calls=%async_computation.7 | async-start | bytes 524288 | tf_op jit(solution)/shard_map/all_to_all | solution.py:63
  158.0 5.4 %all-to-all-done.7 = f32[4,1,16384]{2,1,0:T(1,128)S(1)} async-done(((f32[4,1,16384]{2,1,0:T(1,128)}), f32[4,1,16384]{2,1,0:T(1,128)S(1)}, u32[]{:S(2)}, u32[]{:S(2)}) %all-to-all-start.7) | async-done | bytes 262176 | tf_op jit(solution)/shard_map/all_to_all | solution.py:63
  163.3 1.4 reduce.3
  164.8 2.9 %reshape.272 = f32[512,2,4,16]{3,2,1,0:T(4,128)} reshape(f32[4,16384]{1,0:T(4,128)S(1)} %reduce.3) | data formatting | bytes 524288
  167.6 1.9 copy.43
  172.1 4.6 %collective-permute-start.12 = (f32[2,16,16,128]{3,2,1,0:T(8,128)S(1)}, f32[2,16,16,128]{3,2,1,0:T(8,128)S(1)}, u32[]{:S(2)}, u32[]{:S(2)}) collective-permute-start(f32[2,16,16,128]{3,2,1,0:T(8,128)S(1)} %bitcast.133), channel_id=1, source_target_pairs={{8,0},{16,8},{24,16},{9,1},{17,9},{25,17},{10,2},{18,10},{26,18},{... | collective-permute-start | bytes 786440 | tf_op jit(solution)/shard_map/ppermute | solution.py:30
  176.7 5.5 %collective-permute-start.13 = (f32[2,16,16,128]{3,2,1,0:T(8,128)S(1)}, f32[2,16,16,128]{3,2,1,0:T(8,128)S(1)}, u32[]{:S(2)}, u32[]{:S(2)}) collective-permute-start(f32[2,16,16,128]{3,2,1,0:T(8,128)S(1)} %bitcast.134), channel_id=1, source_target_pairs={{16,0},{24,8},{17,1},{25,9},{18,2},{26,10},{19,3},{27,11},{20,4},{... | collective-permute-start | bytes 786440 | tf_op jit(solution)/shard_map/ppermute | solution.py:30
  (61 shorter events, 19.0 us)
Async XLA Ops:
  0.0 28.0 %copy-start = (f32[2,512,512]{2,1,0:T(8,128)S(1)}, f32[2,512,512]{2,1,0:T(8,128)}, u32[]{:S(2)}) copy-start(f32[2,512,512]{2,1,0:T(8,128)} %param.7) | copy-start | bytes 6291460
  0.0 17.1 %copy-start.1 = (f32[2,16,16,128]{3,2,1,0:T(8,128)S(1)}, f32[2,16,16,128]{3,2,1,0:T(8,128)}, u32[]{:S(2)}) copy-start(f32[2,16,16,128]{3,2,1,0:T(8,128)} %param.6) | copy-start | bytes 786436
  0.9 16.1 %collective-permute-start = (f32[2,1,16,128]{3,1,0,2:T(1,128)S(1)}, f32[2,1,16,128]{3,1,0,2:T(1,128)S(1)}, u32[]{:S(2)}, u32[]{:S(2)}) collective-permute-start(f32[2,1,16,128]{3,1,0,2:T(1,128)S(1)} %copy.23), channel_id=1, source_target_pairs={{0,4},{1,5},{2,6},{3,7},{8,12},{9,13},{10,14},{11,15},{16,20},{17,... | collective-permute-start | bytes 49160 | tf_op jit(solution)/shard_map/ppermute | solution.py:18
  4.4 12.6 %collective-permute-start.2 = (f32[2,1,16,128]{3,1,0,2:T(1,128)S(1)}, f32[2,1,16,128]{3,1,0,2:T(1,128)S(1)}, u32[]{:S(2)}, u32[]{:S(2)}) collective-permute-start(f32[2,1,16,128]{3,1,0,2:T(1,128)S(1)} %copy.26), channel_id=1, source_target_pairs={{4,0},{5,1},{6,2},{7,3},{12,8},{13,9},{14,10},{15,11},{20,16},{21,... | collective-permute-start | bytes 49160 | tf_op jit(solution)/shard_map/ppermute | solution.py:20
  6.7 8.0 %collective-permute-start.1 = (f32[2,1,16,128]{3,1,0,2:T(1,128)S(1)}, f32[2,1,16,128]{3,1,0,2:T(1,128)S(1)}, u32[]{:S(2)}, u32[]{:S(2)}) collective-permute-start(f32[2,1,16,128]{3,1,0,2:T(1,128)S(1)} %get-tuple-element.32), channel_id=1, source_target_pairs={{0,4},{1,5},{2,6},{3,7},{8,12},{9,13},{10,14},{11,15},{16,20},{17,... | collective-permute-start | bytes 49160 | tf_op jit(solution)/shard_map/ppermute | solution.py:18
  11.3 5.6 %collective-permute-start.3 = (f32[2,1,16,128]{3,1,0,2:T(1,128)S(1)}, f32[2,1,16,128]{3,1,0,2:T(1,128)S(1)}, u32[]{:S(2)}, u32[]{:S(2)}) collective-permute-start(f32[2,1,16,128]{3,1,0,2:T(1,128)S(1)} %get-tuple-element.33), channel_id=1, source_target_pairs={{4,0},{5,1},{6,2},{7,3},{12,8},{13,9},{14,10},{15,11},{20,16},{21,... | collective-permute-start | bytes 49160 | tf_op jit(solution)/shard_map/ppermute | solution.py:20
  50.1 3.8 %collective-permute-start.4 = (f32[2,1,16,128]{3,1,0,2:T(1,128)S(1)}, f32[2,1,16,128]{3,1,0,2:T(1,128)S(1)}, u32[]{:S(2)}, u32[]{:S(2)}) collective-permute-start(f32[2,1,16,128]{3,1,0,2:T(1,128)S(1)} %get-tuple-element.24), channel_id=1, source_target_pairs={{0,4},{1,5},{2,6},{3,7},{8,12},{9,13},{10,14},{11,15},{16,20},{17,... | collective-permute-start | bytes 49160 | tf_op jit(solution)/shard_map/ppermute | solution.py:18
  52.5 5.6 %collective-permute-start.5 = (f32[2,1,16,128]{3,1,0,2:T(1,128)S(1)}, f32[2,1,16,128]{3,1,0,2:T(1,128)S(1)}, u32[]{:S(2)}, u32[]{:S(2)}) collective-permute-start(f32[2,1,16,128]{3,1,0,2:T(1,128)S(1)} %get-tuple-element.25), channel_id=1, source_target_pairs={{4,0},{5,1},{6,2},{7,3},{12,8},{13,9},{14,10},{15,11},{20,16},{21,... | collective-permute-start | bytes 49160 | tf_op jit(solution)/shard_map/ppermute | solution.py:20
  90.4 3.1 %collective-permute-start.6 = (f32[2,1,16,128]{3,1,0,2:T(1,128)S(1)}, f32[2,1,16,128]{3,1,0,2:T(1,128)S(1)}, u32[]{:S(2)}, u32[]{:S(2)}) collective-permute-start(f32[2,1,16,128]{3,1,0,2:T(1,128)S(1)} %get-tuple-element.18), channel_id=1, source_target_pairs={{0,4},{1,5},{2,6},{3,7},{8,12},{9,13},{10,14},{11,15},{16,20},{17,... | collective-permute-start | bytes 49160 | tf_op jit(solution)/shard_map/ppermute | solution.py:18
  92.1 5.6 %collective-permute-start.7 = (f32[2,1,16,128]{3,1,0,2:T(1,128)S(1)}, f32[2,1,16,128]{3,1,0,2:T(1,128)S(1)}, u32[]{:S(2)}, u32[]{:S(2)}) collective-permute-start(f32[2,1,16,128]{3,1,0,2:T(1,128)S(1)} %get-tuple-element.19), channel_id=1, source_target_pairs={{4,0},{5,1},{6,2},{7,3},{12,8},{13,9},{14,10},{15,11},{20,16},{21,... | collective-permute-start | bytes 49160 | tf_op jit(solution)/shard_map/ppermute | solution.py:20
  130.0 3.1 %collective-permute-start.8 = (f32[2,1,16,128]{3,1,0,2:T(1,128)S(1)}, f32[2,1,16,128]{3,1,0,2:T(1,128)S(1)}, u32[]{:S(2)}, u32[]{:S(2)}) collective-permute-start(f32[2,1,16,128]{3,1,0,2:T(1,128)S(1)} %get-tuple-element.12), channel_id=1, source_target_pairs={{0,4},{1,5},{2,6},{3,7},{8,12},{9,13},{10,14},{11,15},{16,20},{17,... | collective-permute-start | bytes 49160 | tf_op jit(solution)/shard_map/ppermute | solution.py:18
  131.6 5.6 %collective-permute-start.9 = (f32[2,1,16,128]{3,1,0,2:T(1,128)S(1)}, f32[2,1,16,128]{3,1,0,2:T(1,128)S(1)}, u32[]{:S(2)}, u32[]{:S(2)}) collective-permute-start(f32[2,1,16,128]{3,1,0,2:T(1,128)S(1)} %get-tuple-element.13), channel_id=1, source_target_pairs={{4,0},{5,1},{6,2},{7,3},{12,8},{13,9},{14,10},{15,11},{20,16},{21,... | collective-permute-start | bytes 49160 | tf_op jit(solution)/shard_map/ppermute | solution.py:20
  148.5 8.9 %copy-start.3 = (s32[4]{0:T(128)S(1)}, s32[4]{0:T(128)}, u32[]{:S(2)}) copy-start(s32[4]{0:T(128)} %param.8) | copy-start | bytes 52
  153.9 9.4 %all-to-all-start.7 = ((f32[4,1,16384]{2,1,0:T(1,128)}), f32[4,1,16384]{2,1,0:T(1,128)S(1)}, u32[]{:S(2)}, u32[]{:S(2)}) async-start(f32[4,1,16384]{2,1,0:T(1,128)} %reshape.271), calls=%async_computation.7 | async-start | bytes 524288 | tf_op jit(solution)/shard_map/all_to_all | solution.py:63
  164.8 22.0 %copy-start.2 = (f32[4,4]{1,0:T(4,128)S(1)}, f32[4,4]{1,0:T(4,128)}, u32[]{:S(2)}) copy-start(f32[4,4]{1,0:T(4,128)} %param.9) | copy-start | bytes 196
  169.5 30.8 %collective-permute-start.10 = (f32[2,16,16,128]{3,2,1,0:T(8,128)S(1)}, f32[2,16,16,128]{3,2,1,0:T(8,128)S(1)}, u32[]{:S(2)}, u32[]{:S(2)}) collective-permute-start(f32[2,16,16,128]{3,2,1,0:T(8,128)S(1)} %bitcast.131), channel_id=1, source_target_pairs={{0,16},{8,24},{1,17},{9,25},{2,18},{10,26},{3,19},{11,27},{4,20},{... | collective-permute-start | bytes 786440 | tf_op jit(solution)/shard_map/ppermute | solution.py:30
  170.8 29.5 %collective-permute-start.11 = (f32[2,16,16,128]{3,2,1,0:T(8,128)S(1)}, f32[2,16,16,128]{3,2,1,0:T(8,128)S(1)}, u32[]{:S(2)}, u32[]{:S(2)}) collective-permute-start(f32[2,16,16,128]{3,2,1,0:T(8,128)S(1)} %bitcast.132), channel_id=1, source_target_pairs={{0,8},{8,16},{16,24},{1,9},{9,17},{17,25},{2,10},{10,18},{18,26},{... | collective-permute-start | bytes 786440 | tf_op jit(solution)/shard_map/ppermute | solution.py:30
  172.1 28.2 %collective-permute-start.12 = (f32[2,16,16,128]{3,2,1,0:T(8,128)S(1)}, f32[2,16,16,128]{3,2,1,0:T(8,128)S(1)}, u32[]{:S(2)}, u32[]{:S(2)}) collective-permute-start(f32[2,16,16,128]{3,2,1,0:T(8,128)S(1)} %bitcast.133), channel_id=1, source_target_pairs={{8,0},{16,8},{24,16},{9,1},{17,9},{25,17},{10,2},{18,10},{26,18},{... | collective-permute-start | bytes 786440 | tf_op jit(solution)/shard_map/ppermute | solution.py:30
  176.7 23.7 %collective-permute-start.13 = (f32[2,16,16,128]{3,2,1,0:T(8,128)S(1)}, f32[2,16,16,128]{3,2,1,0:T(8,128)S(1)}, u32[]{:S(2)}, u32[]{:S(2)}) collective-permute-start(f32[2,16,16,128]{3,2,1,0:T(8,128)S(1)} %bitcast.134), channel_id=1, source_target_pairs={{16,0},{24,8},{17,1},{25,9},{18,2},{26,10},{19,3},{27,11},{20,4},{... | collective-permute-start | bytes 786440 | tf_op jit(solution)/shard_map/ppermute | solution.py:30
where the time goes:
time: 203 us; the launch traced here: 201 us
  blocking collectives  59.2 us (29%)
  local copies, waits for them, and re-layouts  50.2 us (25%)
  starting transfers between devices  36.1 us (18%)
  waiting for transfers between devices  20.4 us (10%)
  between operations  17.8 us (9%)
  other arithmetic  8.99 us (4%)
  matrix products  8.52 us (4%)
    all_to_all x4, blocking collectives, local(): lax.all_to_all(source, 'gz', split_axis=2, concat_axis=3, tiled=True)  33.9 us
    unnamed x18, local copies, waits for them, and re-layouts  26.4 us
    all_to_all x3, blocking collectives, local(): lax.all_to_all(solved, 'gz', split_axis=3, concat_axis=2, tiled=True)  25.3 us
    ppermute x5, waiting for transfers between devices, with_halo(): lax.ppermute(head, axis, [((i + 1) % count, i) for i in range(ends)])  14.8 us
    ppermute x5, starting transfers between devices, with_halo(): lax.ppermute(tail, axis, [(i, (i + 1) % count) for i in range(ends)])  13.6 us
    ppermute x4, starting transfers between devices, passed_along(): lax.ppermute(value, axis, [(source, source + steps) for source in range(f...  12.6 us
    dot_general x4, matrix products, local(): jnp.einsum('sij,sabj->sabi', z_inverse, lax.all_to_all(source, 'gz', spli...  8.52 us
    all_to_all x5, local copies, waits for them, and re-layouts, local(): lax.all_to_all(solved, 'gz', split_axis=3, concat_axis=2, tiled=True)  7.99 us
  transfers between devices with their start and end apart: 15, of which 8 were waited for; matrix products, arithmetic and copies ran while one was open for 2% of the time, Pallas kernels for 0%

commit v1 on v0

--- a/solution.py
+++ b/solution.py
@@ -57,7 +57,12 @@
         solved = jnp.einsum(
             "sij,sabj->sabi",
             z_inverse,
-            lax.all_to_all(source, "gz", split_axis=2, concat_axis=3, tiled=True),
+            jnp.concatenate(
+                lax.all_to_all(
+                    jnp.stack(jnp.split(source, lax.axis_size("gz"), axis=2)), "gz", 0, 0
+                ),
+                axis=3,
+            ),
             precision=lax.Precision.HIGHEST,
         )
         state = lax.all_to_all(solved, "gz", split_axis=3, concat_axis=2, tiled=True)

time: 203 us -> 217 us (1.069)
  local copies, waits for them, and re-layouts: 50.2 us -> 61.1 us
  other arithmetic: 8.99 us -> 11.5 us
    slice x1 -> x6, local copies, waits for them, and re-layouts: 0.99 us -> 13.6 us  [reaction(): second = state[1]]
    all_to_all x8 -> x0, local copies, waits for them, and re-layouts: 6.06 us -> none  [local(): lax.all_to_all(source, 'gz', split_axis=2, concat_axis=3, tiled=True)]
    slice x3, local copies, waits for them, and re-layouts: 0.07 us -> 4.63 us  [reaction(): first = state[0]]
where the time goes in v1:
time: 217 us; the launch traced here: 215 us
  local copies, waits for them, and re-layouts  61.1 us (28%)
  blocking collectives  59.2 us (27%)
  starting transfers between devices  36 us (17%)
  waiting for transfers between devices  20.4 us (9%)
  between operations  18.2 us (8%)
  other arithmetic  11.5 us (5%)
  matrix products  8.52 us (4%)
    all_to_all x4, blocking collectives, local(): lax.all_to_all(jnp.stack(jnp.split(source, lax.axis_size('gz'), axis=2)),...  33.9 us
    all_to_all x3, blocking collectives, local(): lax.all_to_all(solved, 'gz', split_axis=3, concat_axis=2, tiled=True)  25.3 us
    unnamed x18, local copies, waits for them, and re-layouts  24.3 us
    ppermute x5, waiting for transfers between devices, with_halo(): lax.ppermute(head, axis, [((i + 1) % count, i) for i in range(ends)])  14.9 us
    slice x6, local copies, waits for them, and re-layouts, reaction(): second = state[1]  13.6 us
    ppermute x5, starting transfers between devices, with_halo(): lax.ppermute(tail, axis, [(i, (i + 1) % count) for i in range(ends)])  13.5 us
    ppermute x4, starting transfers between devices, passed_along(): lax.ppermute(value, axis, [(source, source + steps) for source in range(f...  12.6 us
    dot_general x4, matrix products, local(): jnp.einsum('sij,sabj->sabi', z_inverse, jnp.concatenate(lax.all_to_all(jn...  8.52 us
  transfers between devices with their start and end apart: 15, of which 8 were waited for; matrix products, arithmetic and copies ran while one was open for 2% of the time, Pallas kernels for 0%

profile of v1, /device:TPU:24, one launch (start us, length us, event | category | flops | bytes accessed | tf_op | source)
XLA Modules:
  0.0 215.0 jit_solution(14838405603117446197)
XLA Ops:
  0.9 3.4 %collective-permute-start = (f32[2,1,16,128]{3,2,1,0:T(8,128)S(1)}, f32[2,1,16,128]{3,2,1,0:T(8,128)S(1)}, u32[]{:S(2)}, u32[]{:S(2)}) collective-permute-start(f32[2,1,16,128]{3,2,1,0:T(8,128)S(1)} %get-tuple-element.43), channel_id=1, source_target_pairs={{0,4},{1,5},{2,6},{3,7},{8,12},{9,13},{10,14},{11,15},{16,20},{17,... | collective-permute-start | bytes 49160 | tf_op jit(solution)/shard_map/ppermute | solution.py:18
  6.3 4.5 %collective-permute-start.1 = (f32[2,1,16,128]{3,2,1,0:T(8,128)S(1)}, f32[2,1,16,128]{3,2,1,0:T(8,128)S(1)}, u32[]{:S(2)}, u32[]{:S(2)}) collective-permute-start(f32[2,1,16,128]{3,2,1,0:T(8,128)S(1)} %get-tuple-element.46), channel_id=1, source_target_pairs={{0,4},{1,5},{2,6},{3,7},{8,12},{9,13},{10,14},{11,15},{16,20},{17,... | collective-permute-start | bytes 49160 | tf_op jit(solution)/shard_map/ppermute | solution.py:18
  14.2 2.3 %collective-permute-done.3 = f32[2,1,16,128]{3,2,1,0:T(8,128)S(1)} collective-permute-done((f32[2,1,16,128]{3,2,1,0:T(8,128)S(1)}, f32[2,1,16,128]{3,2,1,0:T(8,128)S(1)}, u32[]{:S(2)}, u32[]{:S(2)}) %collective-permute-start.3) | collective-permute-done | bytes 16416 | tf_op jit(solution)/shard_map/ppermute | solution.py:20
  17.9 8.6 %all_to_all.92 = f32[4,2,16,4,128]{4,3,2,1,0:T(4,128)S(1)} all-to-all(f32[4,2,16,4,128]{4,3,2,1,0:T(4,128)S(1)} %pad_maximum_fusion.10), channel_id=1, replica_groups=mesh['img'=4,'gx'=2,'gz'=4] {'gz'}, dimensions={0} | all-to-all | bytes 524288 | tf_op jit(solution)/shard_map/all_to_all | solution.py:61
  26.8 2.1 fusion.6
  28.9 1.7 copy.21
  30.7 3.1 %reshape.297 = f32[4,1,16384]{2,1,0:T(1,128)S(1)} reshape(f32[512,2,4,16]{3,2,1,0:T(4,128)} %bitcast.110) | data formatting | bytes 524288
  33.7 8.4 %all_to_all.93 = f32[4,1,16384]{2,1,0:T(1,128)S(1)} all-to-all(f32[4,1,16384]{2,1,0:T(1,128)S(1)} %reshape.297), channel_id=1, replica_groups=mesh['img'=4,'gx'=2,'gz'=4] {'gz'}, dimensions={0} | all-to-all | bytes 524288 | tf_op jit(solution)/shard_map/all_to_all | solution.py:68
  44.1 2.8 %reshape.298 = f32[512,2,4,16]{3,2,1,0:T(4,128)} reshape(f32[4,16384]{1,0:T(4,128)S(1)} %reduce) | data formatting | bytes 524288
  47.0 3.0 %fusion.74 = (f32[1,16,4,4,128]{1,3,0,4,2:T(4,128)}, f32[1,16,4,4,128]{1,3,0,4,2:T(4,128)}) fusion(f32[2,16,4,4,128]{1,3,0,4,2:T(4,128)} %bitcast.104), kind=kLoop, calls=%fused_computation.138 | loop fusion | bytes 524288 | tf_op jit(solution)/shard_map/slice | solution.py:35
  50.0 1.9 copy.22
  51.9 1.5 copy.23
  53.4 1.5 copy.24
  55.0 2.3 %collective-permute-start.4 = (f32[2,1,16,128]{3,2,1,0:T(8,128)S(1)}, f32[2,1,16,128]{3,2,1,0:T(8,128)S(1)}, u32[]{:S(2)}, u32[]{:S(2)}) collective-permute-start(f32[2,1,16,128]{3,2,1,0:T(8,128)S(1)} %get-tuple-element.36), channel_id=1, source_target_pairs={{0,4},{1,5},{2,6},{3,7},{8,12},{9,13},{10,14},{11,15},{16,20},{17,... | collective-permute-start | bytes 49160 | tf_op jit(solution)/shard_map/ppermute | solution.py:18
  58.7 4.2 %collective-permute-done.5 = f32[2,1,16,128]{3,2,1,0:T(8,128)S(1)} collective-permute-done((f32[2,1,16,128]{3,2,1,0:T(8,128)S(1)}, f32[2,1,16,128]{3,2,1,0:T(8,128)S(1)}, u32[]{:S(2)}, u32[]{:S(2)}) %collective-permute-start.5) | collective-permute-done | bytes 16416 | tf_op jit(solution)/shard_map/ppermute | solution.py:20
  63.3 8.4 %all_to_all.94 = f32[4,2,16,4,128]{4,3,2,1,0:T(4,128)S(1)} all-to-all(f32[4,2,16,4,128]{4,3,2,1,0:T(4,128)S(1)} %pad_maximum_fusion.11), channel_id=1, replica_groups=mesh['img'=4,'gx'=2,'gz'=4] {'gz'}, dimensions={0} | all-to-all | bytes 524288 | tf_op jit(solution)/shard_map/all_to_all | solution.py:61
  72.0 2.1 fusion.4
  74.1 1.7 copy.26
  75.9 3.1 %reshape.299 = f32[4,1,16384]{2,1,0:T(1,128)S(1)} reshape(f32[512,2,4,16]{3,2,1,0:T(4,128)} %bitcast.111) | data formatting | bytes 524288
  78.9 8.4 %all_to_all.95 = f32[4,1,16384]{2,1,0:T(1,128)S(1)} all-to-all(f32[4,1,16384]{2,1,0:T(1,128)S(1)} %reshape.299), channel_id=1, replica_groups=mesh['img'=4,'gx'=2,'gz'=4] {'gz'}, dimensions={0} | all-to-all | bytes 524288 | tf_op jit(solution)/shard_map/all_to_all | solution.py:68
  88.8 2.8 %reshape.300 = f32[512,2,4,16]{3,2,1,0:T(4,128)} reshape(f32[4,16384]{1,0:T(4,128)S(1)} %reduce.1) | data formatting | bytes 524288
  91.6 3.0 %fusion.73 = (f32[1,16,4,4,128]{1,3,0,4,2:T(4,128)}, f32[1,16,4,4,128]{1,3,0,4,2:T(4,128)}) fusion(f32[2,16,4,4,128]{1,3,0,4,2:T(4,128)} %bitcast.106), kind=kLoop, calls=%fused_computation.137 | loop fusion | bytes 524288 | tf_op jit(solution)/shard_map/slice | solution.py:35
  94.6 1.9 copy.27
  96.5 1.5 copy.28
  98.1 1.5 copy.29
  99.6 1.6 collective-permute-start.6
  102.7 4.2 %collective-permute-done.7 = f32[2,1,16,128]{3,2,1,0:T(8,128)S(1)} collective-permute-done((f32[2,1,16,128]{3,2,1,0:T(8,128)S(1)}, f32[2,1,16,128]{3,2,1,0:T(8,128)S(1)}, u32[]{:S(2)}, u32[]{:S(2)}) %collective-permute-start.7) | collective-permute-done | bytes 16416 | tf_op jit(solution)/shard_map/ppermute | solution.py:20
  107.3 8.4 %all_to_all.96 = f32[4,2,16,4,128]{4,3,2,1,0:T(4,128)S(1)} all-to-all(f32[4,2,16,4,128]{4,3,2,1,0:T(4,128)S(1)} %pad_maximum_fusion.12), channel_id=1, replica_groups=mesh['img'=4,'gx'=2,'gz'=4] {'gz'}, dimensions={0} | all-to-all | bytes 524288 | tf_op jit(solution)/shard_map/all_to_all | solution.py:61
  116.0 2.1 fusion.2
  118.1 1.7 copy.31
  119.8 3.1 %reshape.301 = f32[4,1,16384]{2,1,0:T(1,128)S(1)} reshape(f32[512,2,4,16]{3,2,1,0:T(4,128)} %bitcast.112) | data formatting | bytes 524288
  122.9 8.4 %all_to_all.97 = f32[4,1,16384]{2,1,0:T(1,128)S(1)} all-to-all(f32[4,1,16384]{2,1,0:T(1,128)S(1)} %reshape.301), channel_id=1, replica_groups=mesh['img'=4,'gx'=2,'gz'=4] {'gz'}, dimensions={0} | all-to-all | bytes 524288 | tf_op jit(solution)/shard_map/all_to_all | solution.py:68
  132.7 2.8 %reshape.302 = f32[512,2,4,16]{3,2,1,0:T(4,128)} reshape(f32[4,16384]{1,0:T(4,128)S(1)} %reduce.2) | data formatting | bytes 524288
  135.6 3.0 %fusion.72 = (f32[1,16,4,4,128]{1,3,0,4,2:T(4,128)}, f32[1,16,4,4,128]{1,3,0,4,2:T(4,128)}) fusion(f32[2,16,4,4,128]{1,3,0,4,2:T(4,128)} %bitcast.108), kind=kLoop, calls=%fused_computation.136 | loop fusion | bytes 524288 | tf_op jit(solution)/shard_map/slice | solution.py:35
  138.6 1.9 copy.32
  142.0 1.5 copy.34
  143.6 1.6 collective-permute-start.8
  146.7 4.2 %collective-permute-done.9 = f32[2,1,16,128]{3,2,1,0:T(8,128)S(1)} collective-permute-done((f32[2,1,16,128]{3,2,1,0:T(8,128)S(1)}, f32[2,1,16,128]{3,2,1,0:T(8,128)S(1)}, u32[]{:S(2)}, u32[]{:S(2)}) %collective-permute-start.9) | collective-permute-done | bytes 16416 | tf_op jit(solution)/shard_map/ppermute | solution.py:20
  151.2 8.4 %all_to_all.98 = f32[4,2,16,4,128]{4,3,2,1,0:T(4,128)S(1)} all-to-all(f32[4,2,16,4,128]{4,3,2,1,0:T(4,128)S(1)} %pad_maximum_fusion.13), channel_id=1, replica_groups=mesh['img'=4,'gx'=2,'gz'=4] {'gz'}, dimensions={0} | all-to-all | bytes 524288 | tf_op jit(solution)/shard_map/all_to_all | solution.py:61
  160.0 2.1 fusion
  162.1 1.7 copy.36
  163.8 3.7 %reshape.303 = f32[4,1,16384]{2,1,0:T(1,128)} reshape(f32[512,2,4,16]{3,2,1,0:T(4,128)} %bitcast.113) | data formatting | bytes 524288
  167.5 3.4 %all-to-all-start.7 = ((f32[4,1,16384]{2,1,0:T(1,128)}), f32[4,1,16384]{2,1,0:T(1,128)S(1)}, u32[]{:S(2)}, u32[]{:S(2)}) async-start(f32[4,1,16384]{2,1,0:T(1,128)} %reshape.303), calls=%async_computation.7 | async-start | bytes 524288 | tf_op jit(solution)/shard_map/all_to_all | solution.py:68
  171.6 5.3 %all-to-all-done.7 = f32[4,1,16384]{2,1,0:T(1,128)S(1)} async-done(((f32[4,1,16384]{2,1,0:T(1,128)}), f32[4,1,16384]{2,1,0:T(1,128)S(1)}, u32[]{:S(2)}, u32[]{:S(2)}) %all-to-all-start.7) | async-done | bytes 262176 | tf_op jit(solution)/shard_map/all_to_all | solution.py:68
  178.3 2.8 %reshape.304 = f32[512,2,4,16]{3,2,1,0:T(4,128)} reshape(f32[4,16384]{1,0:T(4,128)S(1)} %reduce.3) | data formatting | bytes 524288
  181.2 1.9 copy.37
  185.7 4.6 %collective-permute-start.12 = (f32[2,16,16,128]{3,2,1,0:T(8,128)S(1)}, f32[2,16,16,128]{3,2,1,0:T(8,128)S(1)}, u32[]{:S(2)}, u32[]{:S(2)}) collective-permute-start(f32[2,16,16,128]{3,2,1,0:T(8,128)S(1)} %bitcast.129), channel_id=1, source_target_pairs={{8,0},{16,8},{24,16},{9,1},{17,9},{25,17},{10,2},{18,10},{26,18},{... | collective-permute-start | bytes 786440 | tf_op jit(solution)/shard_map/ppermute | solution.py:30
  190.3 5.5 %collective-permute-start.13 = (f32[2,16,16,128]{3,2,1,0:T(8,128)S(1)}, f32[2,16,16,128]{3,2,1,0:T(8,128)S(1)}, u32[]{:S(2)}, u32[]{:S(2)}) collective-permute-start(f32[2,16,16,128]{3,2,1,0:T(8,128)S(1)} %bitcast.130), channel_id=1, source_target_pairs={{16,0},{24,8},{17,1},{25,9},{18,2},{26,10},{19,3},{27,11},{20,4},{... | collective-permute-start | bytes 786440 | tf_op jit(solution)/shard_map/ppermute | solution.py:30
  (72 shorter events, 26.5 us)
Async XLA Ops:
  0.0 26.8 %copy-start = (f32[2,512,512]{2,1,0:T(8,128)S(1)}, f32[2,512,512]{2,1,0:T(8,128)}, u32[]{:S(2)}) copy-start(f32[2,512,512]{2,1,0:T(8,128)} %param.7) | copy-start | bytes 6291460
  0.0 17.5 %copy-start.1 = (f32[2,16,16,128]{3,2,1,0:T(8,128)S(1)}, f32[2,16,16,128]{3,2,1,0:T(8,128)}, u32[]{:S(2)}) copy-start(f32[2,16,16,128]{3,2,1,0:T(8,128)} %param.6) | copy-start | bytes 786436
  0.0 17.5 %copy-start.2 = (f32[1,2,16,16,128]{4,3,2,1,0:T(8,128)S(1)}, f32[1,2,16,16,128]{4,3,2,1,0:T(8,128)}, u32[]{:S(2)}) copy-start(f32[1,2,16,16,128]{4,3,2,1,0:T(8,128)} %param.5) | copy-start | bytes 786436
  0.9 12.3 %collective-permute-start = (f32[2,1,16,128]{3,2,1,0:T(8,128)S(1)}, f32[2,1,16,128]{3,2,1,0:T(8,128)S(1)}, u32[]{:S(2)}, u32[]{:S(2)}) collective-permute-start(f32[2,1,16,128]{3,2,1,0:T(8,128)S(1)} %get-tuple-element.43), channel_id=1, source_target_pairs={{0,4},{1,5},{2,6},{3,7},{8,12},{9,13},{10,14},{11,15},{16,20},{17,... | collective-permute-start | bytes 49160 | tf_op jit(solution)/shard_map/ppermute | solution.py:18
  4.3 8.9 %collective-permute-start.2 = (f32[2,1,16,128]{3,2,1,0:T(8,128)S(1)}, f32[2,1,16,128]{3,2,1,0:T(8,128)S(1)}, u32[]{:S(2)}, u32[]{:S(2)}) collective-permute-start(f32[2,1,16,128]{3,2,1,0:T(8,128)S(1)} %get-tuple-element.42), channel_id=1, source_target_pairs={{4,0},{5,1},{6,2},{7,3},{12,8},{13,9},{14,10},{15,11},{20,16},{21,... | collective-permute-start | bytes 49160 | tf_op jit(solution)/shard_map/ppermute | solution.py:20
  6.3 7.9 %collective-permute-start.1 = (f32[2,1,16,128]{3,2,1,0:T(8,128)S(1)}, f32[2,1,16,128]{3,2,1,0:T(8,128)S(1)}, u32[]{:S(2)}, u32[]{:S(2)}) collective-permute-start(f32[2,1,16,128]{3,2,1,0:T(8,128)S(1)} %get-tuple-element.46), channel_id=1, source_target_pairs={{0,4},{1,5},{2,6},{3,7},{8,12},{9,13},{10,14},{11,15},{16,20},{17,... | collective-permute-start | bytes 49160 | tf_op jit(solution)/shard_map/ppermute | solution.py:18
  10.9 5.6 %collective-permute-start.3 = (f32[2,1,16,128]{3,2,1,0:T(8,128)S(1)}, f32[2,1,16,128]{3,2,1,0:T(8,128)S(1)}, u32[]{:S(2)}, u32[]{:S(2)}) collective-permute-start(f32[2,1,16,128]{3,2,1,0:T(8,128)S(1)} %get-tuple-element.47), channel_id=1, source_target_pairs={{4,0},{5,1},{6,2},{7,3},{12,8},{13,9},{14,10},{15,11},{20,16},{21,... | collective-permute-start | bytes 49160 | tf_op jit(solution)/shard_map/ppermute | solution.py:20
  55.0 3.7 %collective-permute-start.4 = (f32[2,1,16,128]{3,2,1,0:T(8,128)S(1)}, f32[2,1,16,128]{3,2,1,0:T(8,128)S(1)}, u32[]{:S(2)}, u32[]{:S(2)}) collective-permute-start(f32[2,1,16,128]{3,2,1,0:T(8,128)S(1)} %get-tuple-element.36), channel_id=1, source_target_pairs={{0,4},{1,5},{2,6},{3,7},{8,12},{9,13},{10,14},{11,15},{16,20},{17,... | collective-permute-start | bytes 49160 | tf_op jit(solution)/shard_map/ppermute | solution.py:18
  57.3 5.6 %collective-permute-start.5 = (f32[2,1,16,128]{3,2,1,0:T(8,128)S(1)}, f32[2,1,16,128]{3,2,1,0:T(8,128)S(1)}, u32[]{:S(2)}, u32[]{:S(2)}) collective-permute-start(f32[2,1,16,128]{3,2,1,0:T(8,128)S(1)} %get-tuple-element.37), channel_id=1, source_target_pairs={{4,0},{5,1},{6,2},{7,3},{12,8},{13,9},{14,10},{15,11},{20,16},{21,... | collective-permute-start | bytes 49160 | tf_op jit(solution)/shard_map/ppermute | solution.py:20
  99.6 3.1 %collective-permute-start.6 = (f32[2,1,16,128]{3,2,1,0:T(8,128)S(1)}, f32[2,1,16,128]{3,2,1,0:T(8,128)S(1)}, u32[]{:S(2)}, u32[]{:S(2)}) collective-permute-start(f32[2,1,16,128]{3,2,1,0:T(8,128)S(1)} %get-tuple-element.28), channel_id=1, source_target_pairs={{0,4},{1,5},{2,6},{3,7},{8,12},{9,13},{10,14},{11,15},{16,20},{17,... | collective-permute-start | bytes 49160 | tf_op jit(solution)/shard_map/ppermute | solution.py:18
  101.3 5.6 %collective-permute-start.7 = (f32[2,1,16,128]{3,2,1,0:T(8,128)S(1)}, f32[2,1,16,128]{3,2,1,0:T(8,128)S(1)}, u32[]{:S(2)}, u32[]{:S(2)}) collective-permute-start(f32[2,1,16,128]{3,2,1,0:T(8,128)S(1)} %get-tuple-element.29), channel_id=1, source_target_pairs={{4,0},{5,1},{6,2},{7,3},{12,8},{13,9},{14,10},{15,11},{20,16},{21,... | collective-permute-start | bytes 49160 | tf_op jit(solution)/shard_map/ppermute | solution.py:20
  143.6 3.1 %collective-permute-start.8 = (f32[2,1,16,128]{3,2,1,0:T(8,128)S(1)}, f32[2,1,16,128]{3,2,1,0:T(8,128)S(1)}, u32[]{:S(2)}, u32[]{:S(2)}) collective-permute-start(f32[2,1,16,128]{3,2,1,0:T(8,128)S(1)} %get-tuple-element.20), channel_id=1, source_target_pairs={{0,4},{1,5},{2,6},{3,7},{8,12},{9,13},{10,14},{11,15},{16,20},{17,... | collective-permute-start | bytes 49160 | tf_op jit(solution)/shard_map/ppermute | solution.py:18
  145.2 5.6 %collective-permute-start.9 = (f32[2,1,16,128]{3,2,1,0:T(8,128)S(1)}, f32[2,1,16,128]{3,2,1,0:T(8,128)S(1)}, u32[]{:S(2)}, u32[]{:S(2)}) collective-permute-start(f32[2,1,16,128]{3,2,1,0:T(8,128)S(1)} %get-tuple-element.21), channel_id=1, source_target_pairs={{4,0},{5,1},{6,2},{7,3},{12,8},{13,9},{14,10},{15,11},{20,16},{21,... | collective-permute-start | bytes 49160 | tf_op jit(solution)/shard_map/ppermute | solution.py:20
  162.1 8.8 %copy-start.4 = (s32[4]{0:T(128)S(1)}, s32[4]{0:T(128)}, u32[]{:S(2)}) copy-start(s32[4]{0:T(128)} %param.8) | copy-start | bytes 52
  167.5 9.4 %all-to-all-start.7 = ((f32[4,1,16384]{2,1,0:T(1,128)}), f32[4,1,16384]{2,1,0:T(1,128)S(1)}, u32[]{:S(2)}, u32[]{:S(2)}) async-start(f32[4,1,16384]{2,1,0:T(1,128)} %reshape.303), calls=%async_computation.7 | async-start | bytes 524288 | tf_op jit(solution)/shard_map/all_to_all | solution.py:68
  178.3 22.4 %copy-start.3 = (f32[4,4]{1,0:T(4,128)S(1)}, f32[4,4]{1,0:T(4,128)}, u32[]{:S(2)}) copy-start(f32[4,4]{1,0:T(4,128)} %param.9) | copy-start | bytes 196
  183.1 31.0 %collective-permute-start.10 = (f32[2,16,16,128]{3,2,1,0:T(8,128)S(1)}, f32[2,16,16,128]{3,2,1,0:T(8,128)S(1)}, u32[]{:S(2)}, u32[]{:S(2)}) collective-permute-start(f32[2,16,16,128]{3,2,1,0:T(8,128)S(1)} %bitcast.127), channel_id=1, source_target_pairs={{0,16},{8,24},{1,17},{9,25},{2,18},{10,26},{3,19},{11,27},{4,20},{... | collective-permute-start | bytes 786440 | tf_op jit(solution)/shard_map/ppermute | solution.py:30
  184.4 29.7 %collective-permute-start.11 = (f32[2,16,16,128]{3,2,1,0:T(8,128)S(1)}, f32[2,16,16,128]{3,2,1,0:T(8,128)S(1)}, u32[]{:S(2)}, u32[]{:S(2)}) collective-permute-start(f32[2,16,16,128]{3,2,1,0:T(8,128)S(1)} %bitcast.128), channel_id=1, source_target_pairs={{0,8},{8,16},{16,24},{1,9},{9,17},{17,25},{2,10},{10,18},{18,26},{... | collective-permute-start | bytes 786440 | tf_op jit(solution)/shard_map/ppermute | solution.py:30
  185.7 28.5 %collective-permute-start.12 = (f32[2,16,16,128]{3,2,1,0:T(8,128)S(1)}, f32[2,16,16,128]{3,2,1,0:T(8,128)S(1)}, u32[]{:S(2)}, u32[]{:S(2)}) collective-permute-start(f32[2,16,16,128]{3,2,1,0:T(8,128)S(1)} %bitcast.129), channel_id=1, source_target_pairs={{8,0},{16,8},{24,16},{9,1},{17,9},{25,17},{10,2},{18,10},{26,18},{... | collective-permute-start | bytes 786440 | tf_op jit(solution)/shard_map/ppermute | solution.py:30
  190.3 23.9 %collective-permute-start.13 = (f32[2,16,16,128]{3,2,1,0:T(8,128)S(1)}, f32[2,16,16,128]{3,2,1,0:T(8,128)S(1)}, u32[]{:S(2)}, u32[]{:S(2)}) collective-permute-start(f32[2,16,16,128]{3,2,1,0:T(8,128)S(1)} %bitcast.130), channel_id=1, source_target_pairs={{16,0},{24,8},{17,1},{25,9},{18,2},{26,10},{19,3},{27,11},{20,4},{... | collective-permute-start | bytes 786440 | tf_op jit(solution)/shard_map/ppermute | solution.py:30
